TPU v7x, 128 devices: a whole 4x4x4 slice. The times are simulated.
128 devices in a mesh: gr: 8 (over z, y_lo), gc: 16 (over x, y_hi, core).
Axes of the slice: x: 4, y: 4 (y_hi: 2, y_lo: 2; y = y_hi * 2 + y_lo), z: 4, core: 2. Of those that a mesh axis runs over, the one named last changes fastest.
Arguments:
- embeddings: bfloat16 [32768, 768], P(('gr', 'gc'))
- cluster_ids: int32 [32768], P(('gr', 'gc')), may hold values from 0 to 7, as said below
Outputs:
- neighbour_sum: float32 [32768, 768], P(('gr', 'gc'))
- density: float32 [32768], P(('gr', 'gc'))
Inputs may be any that keep to these rules, and one draw needn't show every extreme that they name: `cluster_ids`: each device's 256 rows hold exactly 32 rows of every cluster.
All inputs are finite; a program needn't handle non-finite values.
Results may differ from a plain program's by a relative error of at most 0.0017.
Values may be sent and summed in bfloat16 or wider, within the bound.
A program may use at most 128 MiB of HBM per device.

v0:
```python
import jax
import jax.numpy as jnp
from jax import lax
from jax.sharding import PartitionSpec as P

beta_scale = 16.0


def inverse_norms(embeddings):
    wide = embeddings.astype(jnp.float32)
    return lax.rsqrt(jnp.sum(wide * wide, axis=1) + 1e-06)


def kernel_terms(rows, row_inv, cols, col_inv, matched):
    raw = jnp.einsum("rd,cd->rc", rows, cols, preferred_element_type=jnp.float32)
    sim = raw * row_inv[:, None] * col_inv[None, :]
    weight = jnp.exp(beta_scale * (sim - 1.0))
    weight = jnp.where(matched, weight, jnp.float32(0.0))
    dens = jnp.sum(weight, axis=1)
    coef = (weight * col_inv[None, :]).astype(jnp.bfloat16)
    total = jnp.dot(coef, cols, preferred_element_type=jnp.float32)
    return (total, dens)


def make_absorb(rows, row_inv, row_ids, piece):
    cols, col_ids = piece
    col_inv = inverse_norms(cols)
    matched = row_ids[:, None] == col_ids[None, :]
    part_total, part_dens = kernel_terms(rows, row_inv, cols, col_inv, matched)
    return (part_total, part_dens)


def on_device(embeddings, cluster_ids):
    rows, row_ids = (
        lax.all_gather(embeddings, "gc", axis=0, tiled=True),
        lax.all_gather(cluster_ids, "gc", axis=0, tiled=True),
    )
    row_inv = inverse_norms(rows)
    total, dens = make_absorb(
        rows,
        row_inv,
        row_ids,
        (
            lax.all_gather(embeddings, "gr", axis=0, tiled=True),
            lax.all_gather(cluster_ids, "gr", axis=0, tiled=True),
        ),
    )
    neighbour_sum, density = (
        lax.psum_scatter(total, "gc", scatter_dimension=0, tiled=True),
        lax.psum_scatter(dens, "gc", scatter_dimension=0, tiled=True),
    )
    return (neighbour_sum, density)


def solution(mesh):
    in_specs = (P(("gr", "gc"), None), P(("gr", "gc")))
    out_specs = (P(("gr", "gc"), None), P(("gr", "gc")))
    return jax.shard_map(
        on_device, mesh=mesh, in_specs=in_specs, out_specs=out_specs, check_vma=False
    )
```

profile of v0, /device:TPU:1, one launch (start us, length us, event | category | flops | bytes accessed | tf_op | source)
XLA Modules:
  0.0 335.5 jit_solution(5628630368986397603)
XLA Ops:
  7.2 0.0 all-gather.7.cloned.1.call-start
  7.2 0.7 all-gather.7.cloned.1.call-update
  7.9 0.0 all-gather.5.cloned.1.call-start
  7.9 0.7 all-gather.5.cloned.1.call-update
  8.6 0.0 reduce-scatter.2.cloned.1.call-start
  8.7 17.5 %all-gather.1 = s32[8,1,256]{2,1,0:T(1,128)S(1)} all-gather(s32[1,1,256]{2,1,0:T(1,128)} %bitcast.11), channel_id=1, replica_groups=mesh['gr'=8,'gc'=16] {'gr'}, dimensions={0}, use_global_device_ids=true | all-gather | bytes 9216 | tf_op jit(solution)/shard_map/all_gather | solution.py:45
  26.2 28.5 %all-gather = s32[16,1,256]{2,1,0:T(1,128)S(1)} all-gather(s32[1,1,256]{2,1,0:T(1,128)} %bitcast.12), channel_id=1, replica_groups=mesh['gr'=8,'gc'=16] {'gc'}, dimensions={0}, use_global_device_ids=true | all-gather | bytes 17408 | tf_op jit(solution)/shard_map/all_gather | solution.py:36
  54.7 29.8 %all-gather.7.cloned.1.call-done = bf16[2048,768]{1,0:T(8,128)(2,1)} async-done(((bf16[256,768]{1,0:T(8,128)(2,1)}), bf16[2048,768]{1,0:T(8,128)(2,1)}) %all-gather.7.cloned.1.call-update) | async-done | bytes 3145744 | tf_op jit(solution)/shard_map/all_gather | solution.py:44
  84.5 2.6 multiply_reduce_fusion.1
  87.1 64.1 %all-gather.5.cloned.1.call-done = bf16[4096,768]{1,0:T(8,128)(2,1)} async-done(((bf16[256,768]{1,0:T(8,128)(2,1)}), bf16[4096,768]{1,0:T(8,128)(2,1)}) %all-gather.5.cloned.1.call-update) | async-done | bytes 6291472 | tf_op jit(solution)/shard_map/all_gather | solution.py:35
  151.2 4.1 %multiply_reduce_fusion = f32[4096]{0:T(1024)S(1)} fusion(bf16[4096,768]{1,0:T(8,128)(2,1)} %all-gather.5.cloned.1.call-done), kind=kLoop, calls=%fused_computation.4 | loop fusion | flops 9433088 | bytes 6307840 | tf_op jit(solution)/shard_map/reduce_sum | solution.py:11
  155.3 0.0 copy-start
  155.3 25.4 %fusion = (f32[4096]{0:T(1024)S(1)}, f32[4096,2048]{0,1:T(8,128)}) fusion(f32[2048]{0:T(1024)S(1)} %add_rsqrt_fusion.1, f32[4096]{0:T(1024)S(1)} %add_rsqrt_fusion, s32[4096]{0:T(1024)S(1)} %bitcast.7, s32[2048]{0:T(1024)S(1)} %bitcast.9, bf16[4096,768]{1,0:T(8,128)(2,1)} %all-gather.5.cloned.1.call-done, bf16[2048,768]{1,0:T(8,128)(2,1)} %all-gather.7.cloned.1.call-done), kind=kOutput, calls=%fused_computation.2 | convolution fusion | flops 12943618048 | bytes 43057152 | tf_op jit(solution)/shard_map/rd,cd->rc/dot_general | solution.py:15
  180.7 0.0 copy-done
  180.7 0.0 copy-start.1
  180.7 28.3 %fusion.1 = f32[4096,768]{1,0:T(8,128)} fusion(bf16[2048,768]{1,0:T(8,128)(2,1)S(1)} %copy-done, f32[4096,2048]{0,1:T(8,128)} %get-tuple-element.3, f32[2048]{0:T(1024)S(1)} %add_rsqrt_fusion.1, f32[4096]{0:T(1024)S(1)} %add_rsqrt_fusion, s32[4096]{0:T(1024)S(1)} %bitcast.8, s32[2048]{0:T(1024)S(1)} %bitcast.10), kind=kOutput, calls=%fused_computation.3 | convolution fusion | flops 12952010752 | bytes 49332224 | tf_op jit(solution)/shard_map/dot_general | solution.py:21
  209.0 0.0 reduce-scatter.2.cloned.1.call-update
  209.0 0.0 copy-done.1
  209.0 0.6 dynamic-slice
  210.3 61.6 %all-reduce = f32[4096]{0:T(1024)S(1)} all-reduce(f32[4096]{0:T(1024)S(1)} %get-tuple-element.2), channel_id=3, replica_groups=mesh['gr'=8,'gc'=16] {'gc'}, use_global_device_ids=true, to_apply=%region_4.5.clone | all-reduce | flops 4096 | bytes 32768
  271.8 0.6 dynamic-slice.1
  272.5 56.5 %reduce-scatter.2.cloned.1.call-done = f32[256,768]{1,0:T(8,128)} async-done(((f32[4096,768]{1,0:T(8,128)}), f32[256,768]{1,0:T(8,128)}) %reduce-scatter.2.cloned.1.call-update) | async-done | bytes 786448 | tf_op jit(solution)/shard_map/reduce_scatter | solution.py:49
  (2 shorter events, 0.0 us)
Async XLA Ops:
  7.2 77.3 %all-gather.7.cloned.1.call-start = ((), (), s32[]{:S(2)}) async-start(), calls=%async_computation.2 | async-start | bytes 3538944 | tf_op jit(solution)/shard_map/all_gather | solution.py:44
  7.9 143.3 %all-gather.5.cloned.1.call-start = ((), (), s32[]{:S(2)}) async-start(), calls=%async_computation.1 | async-start | bytes 6684672 | tf_op jit(solution)/shard_map/all_gather | solution.py:35
  8.6 320.3 %reduce-scatter.2.cloned.1.call-start = ((), (), s32[]{:S(2)}) async-start(), calls=%async_computation.3 | async-start | bytes 13369344 | tf_op jit(solution)/shard_map/reduce_scatter | solution.py:49
  155.3 25.4 %copy-start = (bf16[2048,768]{1,0:T(8,128)(2,1)S(1)}, bf16[2048,768]{1,0:T(8,128)(2,1)}, u32[]{:S(2)}) copy-start(bf16[2048,768]{1,0:T(8,128)(2,1)} %all-gather.7.cloned.1.call-done) | copy-start | bytes 9437188
  180.7 28.3 %copy-start.1 = (u32[128]{0:T(128)S(1)}, u32[128]{0:T(128)}, u32[]{:S(2)}) copy-start(u32[128]{0:T(128)} %constant.12) | copy-start | bytes 1540
Sparse Core Ops, SparseCore 0:
  9.6 74.7 all-gather.6
  86.9 64.2 all-gather.4
  209.1 119.8 reduce-scatter.1
where the time goes:
time: 336 us
  waiting for transfers between devices  152 us (45%)
  blocking collectives  108 us (32%)
  matrix products  53.7 us (16%)
  between operations  14.4 us (4%)
  other arithmetic  6.67 us (2%)
    all_gather x1, waiting for transfers between devices, on_device(): lax.all_gather(embeddings, 'gc', axis=0, tiled=True)  64.1 us
    unnamed x1, blocking collectives  61.6 us
    reduce_scatter x1, waiting for transfers between devices, on_device(): lax.psum_scatter(total, 'gc', scatter_dimension=0, tiled=True)  56.5 us
    all_gather x1, waiting for transfers between devices, on_device(): lax.all_gather(embeddings, 'gr', axis=0, tiled=True)  29.8 us
    all_gather x1, blocking collectives, on_device(): lax.all_gather(cluster_ids, 'gc', axis=0, tiled=True)  28.5 us
    dot_general x1, matrix products, kernel_terms(): total = jnp.dot(coef, cols, preferred_element_type=jnp.float32)  28.3 us
    dot_general x1, matrix products, kernel_terms(): jnp.einsum('rd,cd->rc', rows, cols, preferred_element_type=jnp.float32)  25.4 us
    all_gather x1, blocking collectives, on_device(): lax.all_gather(cluster_ids, 'gr', axis=0, tiled=True)  17.5 us
  transfers between devices with their start and end apart: 3, of which 3 were waited for; matrix products, arithmetic and copies ran while one was open for 1% of the time, Pallas kernels for 0%

commit v1 on v0

v1 whole, which is shorter than its diff:
```python
import functools

import jax
import jax.numpy as jnp
from jax import lax
from jax.experimental import pallas as pl
from jax.experimental.pallas import tpu as pltpu
from jax.sharding import PartitionSpec as P

MESH = pl.DeviceIdType.MESH
F32 = jnp.float32
BF16 = jnp.bfloat16

beta_scale = 16.0
ROWS = 256
D = 768
PARTS = 3
W = D // PARTS
SLICE = 32
HALF = ROWS // 2
ORDER = (0, 1, 2, 4, 3, 5, 6, 7)


def place():
    gr, gc = lax.axis_index("gr"), lax.axis_index("gc")
    x = gc // 4
    y = ((gc // 2) % 2) * 2 + gr % 2
    z = gr // 2
    return x, y, z, gc % 2


def device(x, y, z, core):
    return (z * 2 + y % 2, x * 4 + (y // 2) * 2 + core)


def near(v):
    return v + 1 - 2 * (v % 2)


def far(v):
    return 3 - v


def link_items():
    items = [[(b, 0), ((b + 2) % 3, 0), ((b + 1) % 3, 0)] for b in range(3)]
    for b in range(3):
        p1, p2 = (b + 2) % 3, (b + 1) % 3
        b1, b2 = 1 << p1, 1 << p2
        items[b] += [(p1, b1), (p2, b2), (p2, b1), (p2, b1 | b2)]
    return items


def to_lanes(column):
    return jnp.transpose(jnp.broadcast_to(column, (column.shape[0], 128)))[0:1, :]


def to_column(row):
    return jnp.transpose(jnp.broadcast_to(row, (128, row.shape[1])))[:, 0:1]


def kernel(
    e_ref, ids_ref, out_ref, dens_ref,
    sorted_ref, held, acc, dacc, perm, perm_t, inv_ref, coded, pay, back, back_pay,
    deliver_send, deliver_recv, link_send, link_recv, core_send, core_recv,
    ret_send, ret_recv, pay_send, pay_recv,
):
    x, y, z, core = place()
    here = (x, y, z)
    outer = []
    for s in range(8):
        t = [far(here[a]) if (ORDER[s] >> a) & 1 else here[a] for a in range(3)]
        outer.append(device(*t, core))
    inner = []
    for a in range(3):
        t = [near(here[i]) if i == a else here[i] for i in range(3)]
        inner.append(device(*t, core))
    sibling = device(x, y, z, 1 - core)

    barrier = pltpu.get_barrier_semaphore()
    for d in outer[1:] + inner + [sibling]:
        pl.semaphore_signal(barrier, inc=1, device_id=d, device_id_type=MESH)

    mine = x // 2 + 2 * (y // 2) + 4 * (z // 2)
    rel = jnp.bitwise_xor(ids_ref[...], mine)
    slot = jnp.where(rel == 3, 4, jnp.where(rel == 4, 3, rel)).astype(F32)
    slot_col = to_column(slot)
    i0 = lax.broadcasted_iota(jnp.int32, (ROWS, ROWS), 0)
    i1 = lax.broadcasted_iota(jnp.int32, (ROWS, ROWS), 1)
    earlier = jnp.where((slot_col == slot) & (i0 < i1), F32(1.0), F32(0.0))
    pos = slot * SLICE + jnp.sum(earlier, axis=0, keepdims=True)
    p = jnp.where(i0.astype(F32) == pos, F32(1.0), F32(0.0)).astype(BF16)
    perm[...] = p
    for part in range(PARTS):
        rows = jnp.dot(p, e_ref[:, part * W:(part + 1) * W], preferred_element_type=F32).astype(BF16)
        sorted_ref[part] = rows
        held[0, part, 0, 0:SLICE, :] = rows[0:SLICE]

    pl.semaphore_wait(barrier, 11)

    def deliver(s):
        return pltpu.make_async_remote_copy(
            src_ref=sorted_ref.at[:, pl.ds(s * SLICE, SLICE), :],
            dst_ref=held.at[0, :, 0, pl.ds(s * SLICE, SLICE), :],
            send_sem=deliver_send.at[s], recv_sem=deliver_recv.at[s],
            device_id=outer[s], device_id_type=MESH)

    items = link_items()

    def over_link(b, k, half):
        part, h = items[b][k]
        rows = pl.ds(half * HALF, HALF)
        return pltpu.make_async_remote_copy(
            src_ref=held.at[0, part, h, rows, :],
            dst_ref=held.at[0, part, h ^ (1 << b), rows, :],
            send_sem=link_send.at[b, k, half], recv_sem=link_recv.at[b, k, half],
            device_id=inner[b], device_id_type=MESH)

    def to_sibling(h):
        return pltpu.make_async_remote_copy(
            src_ref=held.at[0, :, h], dst_ref=held.at[1, :, h],
            send_sem=core_send.at[h], recv_sem=core_recv.at[h],
            device_id=sibling, device_id_type=MESH)

    def arrive(b, k, half):
        over_link(b, k, half).wait_recv()
        part, h = items[b][k]
        h ^= 1 << b
        for d in range(3):
            if (part, h) in items[d]:
                over_link(d, items[d].index((part, h)), half).start()

    def absorb(c, h, first=False):
        cols = [held[c, part, h] for part in range(PARTS)]
        raw = None
        squares = None
        for part in range(PARTS):
            r = lax.dot_general(held[0, part, 0], cols[part], (((1,), (1,)), ((), ())),
                                preferred_element_type=F32)
            wide = cols[part].astype(F32)
            q = jnp.sum(wide * wide, axis=1, keepdims=True)
            raw = r if raw is None else raw + r
            squares = q if squares is None else squares + q
        inv = lax.rsqrt(squares + 1e-06)
        if first:
            inv_ref[...] = jnp.broadcast_to(inv, (ROWS, 128))
        inv_lanes = to_lanes(inv)
        sim = raw * inv_ref[:, 0:1] * inv_lanes
        weight = jnp.exp(beta_scale * (sim - 1.0))
        dens = weight[:, :128] + weight[:, 128:]
        coef = (weight * inv_lanes).astype(BF16)
        dacc[...] = dens if first else dacc[...] + dens
        for part in range(PARTS):
            at = slice(part * W, (part + 1) * W)
            add = jnp.dot(coef, cols[part], preferred_element_type=F32)
            acc[:, at] = add if first else acc[:, at] + add

    for s in range(1, 8):
        deliver(s).start()
    perm_t[...] = jnp.where(i1.astype(F32) == to_column(pos), F32(1.0), F32(0.0))
    for s in range(1, 4):
        deliver(s).wait_recv()
    for k in range(3):
        for b in range(3):
            over_link(b, k, 0).start()
    for s in range(4, 8):
        deliver(s).wait_recv()
    for k in range(3):
        for b in range(3):
            over_link(b, k, 1).start()
    to_sibling(0).start()
    absorb(0, 0, first=True)
    for k in range(3):
        for b in range(3):
            arrive(b, k, 0)
    to_sibling(0).wait_recv()
    absorb(1, 0)
    for k in range(3):
        for b in range(3):
            arrive(b, k, 1)
    for b in range(3):
        to_sibling(1 << b).start()
    todo = [(c, 1 << b) for c in range(2) for b in range(3)]
    for k in range(3, 6):
        for half in range(2):
            for b in range(3):
                arrive(b, k, half)
            c, h = todo.pop(0)
            if c == 1:
                to_sibling(h).wait_recv()
            absorb(c, h)
    pairs = (3, 5, 6)
    for h in pairs:
        to_sibling(h).start()
    for c in range(2):
        for h in pairs:
            if c == 1:
                to_sibling(h).wait_recv()
            absorb(c, h)
            if c == 1 and h == 3:
                for half in range(2):
                    for b in range(3):
                        arrive(b, 6, half)
                to_sibling(7).start()
    absorb(0, 7)
    to_sibling(7).wait_recv()
    absorb(1, 7)

    total = acc[...]
    top = jnp.max(jnp.abs(total), axis=1, keepdims=True)
    scale = (jnp.maximum(top, 1e-30) * (1.015625 / 32767.0)).astype(BF16).astype(F32)
    dens_col = jnp.sum(dacc[...], axis=1, keepdims=True)
    pay[0:1, :] = to_lanes(dens_col)
    pay[1:2, :] = to_lanes(scale)
    coded[...] = jnp.floor(total * (1.0 / scale) + 0.5).astype(jnp.int32).astype(jnp.int16)

    def give_back(s):
        return pltpu.make_async_remote_copy(
            src_ref=coded.at[pl.ds(s * SLICE, SLICE), :],
            dst_ref=back.at[pl.ds(s * SLICE, SLICE), :],
            send_sem=ret_send.at[s], recv_sem=ret_recv.at[s],
            device_id=outer[s], device_id_type=MESH)

    def give_pay(s):
        return pltpu.make_async_remote_copy(
            src_ref=pay, dst_ref=back_pay.at[s],
            send_sem=pay_send.at[s], recv_sem=pay_recv.at[s],
            device_id=outer[s], device_id_type=MESH)

    for s in range(7, 0, -1):
        give_back(s).start()
        give_pay(s).start()
    back[0:SLICE, :] = coded[0:SLICE, :]
    back_pay[0] = pay[...]
    for s in range(7, 0, -1):
        give_pay(s).wait_recv()

    block = lax.broadcasted_iota(jnp.int32, (8, ROWS), 1) // SLICE
    got = jnp.zeros((8, ROWS), F32)
    for s in range(8):
        got = jnp.where(block == s, back_pay[s], got)
    dens_row, scale_row = got[0:1, :], got[1:2, :]
    d1 = dens_row.astype(BF16)
    rest = dens_row - d1.astype(F32)
    d2 = rest.astype(BF16)
    d3 = (rest - d2.astype(F32)).astype(BF16)
    lift = lambda v: jnp.broadcast_to(v.astype(F32), (16, ROWS))
    which = lax.broadcasted_iota(jnp.int32, (16, ROWS), 0)
    terms = jnp.where(which == 0, lift(d1), jnp.where(which == 1, lift(d2), jnp.where(which == 2, lift(d3), F32(0.0))))
    spread = jnp.dot(terms.astype(BF16), perm[...], preferred_element_type=F32)
    dens_ref[...] = jnp.sum(spread, axis=0, keepdims=True)
    placed = (perm_t[...] * scale_row).astype(BF16)

    for s in range(7, 0, -1):
        give_back(s).wait_recv()
    for part in range(PARTS):
        at = slice(part * W, (part + 1) * W)
        value = back[:, at].astype(jnp.int32).astype(F32)
        high = value.astype(BF16)
        low = (value - high.astype(F32)).astype(BF16)
        out_ref[:, at] = jnp.dot(placed, high, preferred_element_type=F32) + jnp.dot(
            placed, low, preferred_element_type=F32)

    for s in range(1, 8):
        deliver(s).wait_send()
        give_back(s).wait_send()
        give_pay(s).wait_send()
    for b in range(3):
        for k in range(7):
            for half in range(2):
                over_link(b, k, half).wait_send()
    for h in range(8):
        to_sibling(h).wait_send()


def on_device(embeddings, cluster_ids):
    dma = pltpu.SemaphoreType.DMA
    total, dens = pl.pallas_call(
        kernel,
        out_shape=(jax.ShapeDtypeStruct((ROWS, D), F32), jax.ShapeDtypeStruct((1, ROWS), F32)),
        in_specs=[pl.BlockSpec(memory_space=pltpu.VMEM)] * 2,
        out_specs=(pl.BlockSpec(memory_space=pltpu.VMEM), pl.BlockSpec(memory_space=pltpu.VMEM)),
        scratch_shapes=[
            pltpu.VMEM((PARTS, ROWS, W), BF16),
            pltpu.VMEM((2, PARTS, 8, ROWS, W), BF16),
            pltpu.VMEM((ROWS, D), F32),
            pltpu.VMEM((ROWS, 128), F32),
            pltpu.VMEM((ROWS, ROWS), BF16),
            pltpu.VMEM((ROWS, ROWS), F32),
            pltpu.VMEM((ROWS, 128), F32),
            pltpu.VMEM((ROWS, D), jnp.int16),
            pltpu.VMEM((8, ROWS), F32),
            pltpu.VMEM((ROWS, D), jnp.int16),
            pltpu.VMEM((8, 8, ROWS), F32),
            dma((8,)), dma((8,)),
            dma((3, 7, 2)), dma((3, 7, 2)),
            dma((8,)), dma((8,)),
            dma((8,)), dma((8,)),
            dma((8,)), dma((8,)),
        ],
        compiler_params=pltpu.CompilerParams(
            collective_id=0, has_side_effects=True, vmem_limit_bytes=40 * 1024 * 1024),
        cost_estimate=pl.CostEstimate(
            flops=4 * ROWS * 4096 * D, bytes_accessed=3 * ROWS * D * 2, transcendentals=ROWS * 4096),
    )(embeddings, cluster_ids.reshape(1, ROWS))
    return total, dens.reshape(ROWS)


def solution(mesh):
    in_specs = (P(("gr", "gc"), None), P(("gr", "gc")))
    out_specs = (P(("gr", "gc"), None), P(("gr", "gc")))
    return jax.shard_map(
        on_device, mesh=mesh, in_specs=in_specs, out_specs=out_specs, check_vma=False
    )
```

time: 336 us -> 51.6 us (0.15)
  waiting for transfers between devices: 152 us -> 0 us
  blocking collectives: 108 us -> 0 us
  matrix products: 53.7 us -> 0 us
  Pallas kernels: 0 us -> 47.7 us
  between operations: 14.4 us -> 0.65 us
  other arithmetic: 6.67 us -> 0 us
    all_gather x2 -> x0, waiting for transfers between devices: 93.9 us -> none  [the longest x1 64.1 us: on_device(): lax.all_gather(embeddings, 'gc', axis=0, tiled=True)]
    unnamed x1 -> x0, blocking collectives: 61.6 us -> none
    reduce_scatter x1 -> x0, waiting for transfers between devices: 56.5 us -> none  [on_device(): lax.psum_scatter(total, 'gc', scatter_dimension=0, tiled=True)]
    dot_general x2 -> x0, matrix products: 53.7 us -> none  [the longest x1 28.3 us: kernel_terms(): total = jnp.dot(coef, cols, preferred_element_type=jnp.float32)]
    pallas_call x0 -> x1, Pallas kernels: none -> 47.7 us  [on_device(): pl.pallas_call(kernel, out_shape=(jax.ShapeDtypeStruct((ROWS, D), F32), j...]
    all_gather x2 -> x0, blocking collectives: 46 us -> none  [the longest x1 28.5 us: on_device(): lax.all_gather(cluster_ids, 'gc', axis=0, tiled=True)]
    reduce_sum x2 -> x0, other arithmetic: 6.66 us -> none  [inverse_norms(): return lax.rsqrt(jnp.sum(wide * wide, axis=1) + 1e-06)]
  transfers between devices with their start and end apart: 3 -> 0, of which waited for: 3 -> 0; matrix products, arithmetic and copies ran while one was open for 1% -> 0% of each run, Pallas kernels for 0% -> 0%
where the time goes in v1:
time: 51.6 us; the launch traced here: 51.4 us
  Pallas kernels  47.7 us (92%)
  local copies, waits for them, and re-layouts  3.11 us (6%)
  between operations  0.65 us (1%)
    pallas_call x1, Pallas kernels, on_device(): pl.pallas_call(kernel, out_shape=(jax.ShapeDtypeStruct((ROWS, D), F32), j...  47.7 us
    unnamed x6, local copies, waits for them, and re-layouts  3.11 us

profile of v1, /device:TPU:1, one launch (start us, length us, event | category | flops | bytes accessed | tf_op | source)
XLA Modules:
  0.0 51.4 jit_solution(14633093524223291148)
XLA Ops:
  0.6 0.0 copy-start.1
  0.6 0.7 %copy-done.1 = s32[256]{0:T(256)S(1)} copy-done((s32[256]{0:T(256)S(1)}, s32[256]{0:T(256)}, u32[]{:S(2)}) %copy-start.1) | copy-done | bytes 1048
  1.3 0.0 copy-start
  1.3 1.0 %copy-done = bf16[256,768]{1,0:T(8,128)(2,1)S(1)} copy-done((bf16[256,768]{1,0:T(8,128)(2,1)S(1)}, bf16[256,768]{1,0:T(8,128)(2,1)}, u32[]{:S(2)}) %copy-start) | copy-done | bytes 393240
  2.3 47.7 %shard_map.41 = (f32[256,768]{1,0:T(8,128)S(1)}, f32[1,256]{1,0:T(1,128)S(1)}) custom-call(bf16[256,768]{1,0:T(8,128)(2,1)S(1)} %copy-done, s32[1,256]{1,0:T(1,128)S(1)} %bitcast.3), custom_call_target="tpu_custom_call" | custom-call | flops 3221225472 | bytes 1179648 | tf_op jit(solution)/shard_map/pallas_call | solution.py:277
  50.0 0.9 %copy.6 = f32[256,768]{1,0:T(8,128)} copy(f32[256,768]{1,0:T(8,128)S(1)} %get-tuple-element.8) | data formatting | bytes 1572864
  50.9 0.6 %copy.7 = f32[256]{0:T(256)} copy(f32[256]{0:T(256)S(1)} %bitcast.2) | data formatting | bytes 2048
Async XLA Ops:
  0.6 0.7 %copy-start.1 = (s32[256]{0:T(256)S(1)}, s32[256]{0:T(256)}, u32[]{:S(2)}) copy-start(s32[256]{0:T(256)} %param.3) | copy-start | bytes 3076
  1.3 1.0 %copy-start = (bf16[256,768]{1,0:T(8,128)(2,1)S(1)}, bf16[256,768]{1,0:T(8,128)(2,1)}, u32[]{:S(2)}) copy-start(bf16[256,768]{1,0:T(8,128)(2,1)} %e_ref.1) | copy-start | bytes 1179652

commit v2 on v0

v2 whole, which is shorter than its diff:
```python
import functools

import jax
import jax.numpy as jnp
from jax import lax
from jax.experimental import pallas as pl
from jax.experimental.pallas import tpu as pltpu
from jax.sharding import PartitionSpec as P

MESH = pl.DeviceIdType.MESH
F32 = jnp.float32
BF16 = jnp.bfloat16

beta_scale = 16.0
ROWS = 256
D = 768
PARTS = 2
W = D // PARTS
SLICE = 32
HALF = ROWS // 2
SPLIT = 2
GROUPS = ((0, 32), (32, 96), (128, 128))
ORDER = (0, 1, 2, 4, 3, 5, 6, 7)


def place():
    gr, gc = lax.axis_index("gr"), lax.axis_index("gc")
    x = gc // 4
    y = ((gc // 2) % 2) * 2 + gr % 2
    z = gr // 2
    return x, y, z, gc % 2


def device(x, y, z, core):
    return (z * 2 + y % 2, x * 4 + (y // 2) * 2 + core)


def near(v):
    return v + 1 - 2 * (v % 2)


def far(v):
    return 3 - v


ITEMS = (((0, 0), (1, 0), (1, 2)), ((1, 0), (0, 0), (0, 1)))


def to_lanes(column):
    return jnp.transpose(jnp.broadcast_to(column, (column.shape[0], 128)))[0:1, :]


def to_column(row):
    return jnp.transpose(jnp.broadcast_to(row, (128, row.shape[1])))[:, 0:1]


def kernel(
    e_hbm, ids_hbm, out_ref, dens_ref,
    e_ref, ids_ref, load_sem, sorted_ref, held, across_rows, acc, dacc, perm, perm_t, inv_ref, coded, pay, back, back_pay,
    deliver_send, deliver_recv, link_send, link_recv, core_send, core_recv,
    ret_send, ret_recv, pay_send, pay_recv,
):
    x, y, z, core = place()
    here = (x, y, z)
    outer = []
    for s in range(8):
        t = [far(here[a]) if (ORDER[s] >> a) & 1 else here[a] for a in range(3)]
        outer.append(device(*t, core))
    inner = []
    for a in range(3):
        t = [near(here[i]) if i == a else here[i] for i in range(3)]
        inner.append(device(*t, core))
    sibling = device(x, y, z, 1 - core)
    across = []
    for s in range(8):
        t = [far(here[a]) if (ORDER[s] >> a) & 1 else here[a] for a in range(3)]
        t[SPLIT] = near(t[SPLIT])
        across.append(device(*t, core))
    holders = (outer, across)

    barrier = pltpu.get_barrier_semaphore()
    for d in outer[1:] + inner + [sibling] + across[1:]:
        pl.semaphore_signal(barrier, inc=1, device_id=d, device_id_type=MESH)

    loads = [pltpu.make_async_copy(ids_hbm, ids_ref, load_sem.at[0]),
             pltpu.make_async_copy(e_hbm, e_ref, load_sem.at[1])]
    for load in loads:
        load.start()

    mine = x // 2 + 2 * (y // 2) + 4 * (z // 2)
    loads[0].wait()
    rel = jnp.bitwise_xor(ids_ref[...], mine)
    slot = jnp.where(rel == 3, 4, jnp.where(rel == 4, 3, rel)).astype(F32)
    slot_col = to_column(slot)
    i0 = lax.broadcasted_iota(jnp.int32, (ROWS, ROWS), 0)
    i1 = lax.broadcasted_iota(jnp.int32, (ROWS, ROWS), 1)
    earlier = jnp.where((slot_col == slot) & (i0 < i1), F32(1.0), F32(0.0))
    pos = slot * SLICE + jnp.sum(earlier, axis=0, keepdims=True)
    p = jnp.where(i0.astype(F32) == pos, F32(1.0), F32(0.0)).astype(BF16)
    perm[...] = p
    loads[1].wait()
    rows = jnp.dot(p, e_ref[...], preferred_element_type=F32).astype(BF16)
    sorted_ref[...] = rows
    held[0, 0, 0:SLICE, :] = rows[0:SLICE]

    pl.semaphore_wait(barrier, 18)

    def deliver(s):
        return pltpu.make_async_remote_copy(
            src_ref=sorted_ref.at[pl.ds(s * SLICE, SLICE), :],
            dst_ref=held.at[0, 0, pl.ds(s * SLICE, SLICE), :],
            send_sem=deliver_send.at[s], recv_sem=deliver_recv.at[s],
            device_id=outer[s], device_id_type=MESH)

    def over_link(b, k, g):
        rows = pl.ds(*GROUPS[g])
        if b == SPLIT:
            source, target = held.at[0, 0, rows, :], across_rows.at[rows, :]
        else:
            part, h = ITEMS[b][k]
            cols = pl.ds(part * W, W)
            source, target = held.at[0, h, rows, cols], held.at[0, h ^ (1 << b), rows, cols]
        return pltpu.make_async_remote_copy(
            src_ref=source, dst_ref=target,
            send_sem=link_send.at[b, k, g], recv_sem=link_recv.at[b, k, g],
            device_id=inner[b], device_id_type=MESH)

    def to_sibling(h, half):
        rows = pl.ds(half * HALF, HALF)
        return pltpu.make_async_remote_copy(
            src_ref=held.at[0, h, rows, :], dst_ref=held.at[1, h, rows, :],
            send_sem=core_send.at[h, half], recv_sem=core_recv.at[h, half],
            device_id=sibling, device_id_type=MESH)

    def piece_to_sibling(part, h, g):
        rows, cols = pl.ds(*GROUPS[g]), pl.ds(part * W, W)
        return pltpu.make_async_remote_copy(
            src_ref=held.at[0, h, rows, cols], dst_ref=held.at[1, h, rows, cols],
            send_sem=core_send.at[h, g // 2], recv_sem=core_recv.at[h, g // 2],
            device_id=sibling, device_id_type=MESH)

    def arrive(b, k, g):
        over_link(b, k, g).wait_recv()
        part, h = ITEMS[b][k]
        h ^= 1 << b
        if (part, h) in ITEMS[1 - b]:
            over_link(1 - b, ITEMS[1 - b].index((part, h)), g).start()
        piece_to_sibling(part, h, g).start()

    def row_inv(rows):
        wide = rows.astype(F32)
        return lax.rsqrt(jnp.sum(wide * wide, axis=1, keepdims=True) + 1e-06)

    def absorb(pieces, sides, first=False, steps=None):
        cols = jnp.concatenate([held[c, h, half * HALF:(half + 1) * HALF, :] for c, h, half in pieces], axis=0)
        inv_lanes = to_lanes(row_inv(cols))
        for side, start, size in steps or [(side, 0, ROWS) for side in sides]:
            own = slice(start, start + size)
            rows = slice(side * ROWS + start, side * ROWS + start + size)
            mine = held[0, 0, own, :] if side == 0 else across_rows[own, :]
            if first:
                inv_ref[rows, :] = jnp.broadcast_to(row_inv(mine), (size, 128))
            raw = lax.dot_general(mine, cols, (((1,), (1,)), ((), ())), preferred_element_type=F32)
            sim = raw * inv_ref[rows, 0:1] * inv_lanes
            weight = jnp.exp(beta_scale * (sim - 1.0))
            dens = weight[:, :128] + weight[:, 128:]
            coef = (weight * inv_lanes).astype(BF16)
            dacc[rows, :] = dens if first else dacc[rows, :] + dens
            add = jnp.dot(coef, cols, preferred_element_type=F32)
            acc[rows, :] = add if first else acc[rows, :] + add
            if steps:
                finish(side, start // HALF)

    def give_back(side, s):
        return pltpu.make_async_remote_copy(
            src_ref=coded.at[side, pl.ds(s * SLICE, SLICE), :],
            dst_ref=back.at[side, pl.ds(s * SLICE, SLICE), :],
            send_sem=ret_send.at[side, s], recv_sem=ret_recv.at[side, s],
            device_id=holders[side][s], device_id_type=MESH)

    def give_pay(side, s):
        return pltpu.make_async_remote_copy(
            src_ref=pay.at[side, s // 4], dst_ref=back_pay.at[side, s],
            send_sem=pay_send.at[side, s], recv_sem=pay_recv.at[side, s],
            device_id=holders[side][s], device_id_type=MESH)

    def leaves(side, s):
        return side == 1 or s > 0

    def finish(side, half):
        own = slice(half * HALF, (half + 1) * HALF)
        rows = slice(side * ROWS + half * HALF, side * ROWS + (half + 1) * HALF)
        total = acc[rows, :]
        top = jnp.max(jnp.abs(total), axis=1, keepdims=True)
        scale = (jnp.maximum(top, 1e-30) * (1.015625 / 32767.0)).astype(BF16).astype(F32)
        coded[side, own, :] = jnp.floor(total * (1.0 / scale) + 0.5).astype(jnp.int32).astype(jnp.int16)
        dens_col = jnp.sum(dacc[rows, :], axis=1, keepdims=True)
        pay[side, half, 0:1, :] = to_lanes(dens_col)
        pay[side, half, 1:2, :] = to_lanes(scale)
        for s in range(4 * half + 3, 4 * half - 1, -1):
            if leaves(side, s):
                give_back(side, s).start()
                give_pay(side, s).start()

    for s in range(1, 4):
        deliver(s).start()
    perm_t[...] = jnp.where(i1.astype(F32) == to_column(pos), F32(1.0), F32(0.0))
    def own(g):
        for k in range(2):
            for b in range(2):
                over_link(b, k, g).start()
            if k == 0:
                over_link(SPLIT, 0, g).start()

    def arrivals(ks, g):
        for k in ks:
            for b in range(2):
                arrive(b, k, g)

    def whole(c, h):
        return (c, h, 0), (c, h, 1)

    own(0)
    for s in range(1, 4):
        deliver(s).wait_send()
    for s in range(4, 8):
        deliver(s).start()
    for s in range(1, 4):
        deliver(s).wait_recv()
    own(1)
    to_sibling(0, 0).start()
    arrivals(range(2), 0)
    arrivals(range(2), 1)
    for s in range(4, 8):
        deliver(s).wait_recv()
    own(2)
    to_sibling(0, 1).start()
    absorb(whole(0, 0), (0,), first=True)
    arrivals((2,), 0)
    to_sibling(0, 0).wait_recv()
    to_sibling(0, 1).wait_recv()
    absorb(whole(1, 0), (0,))
    arrivals((2,), 1)
    for g in range(3):
        over_link(SPLIT, 0, g).wait_recv()
    absorb(whole(0, 0), (1,), first=True)
    arrivals(range(2), 2)
    absorb(whole(1, 0), (1,))
    absorb(whole(0, 1), (0, 1))
    absorb(whole(0, 2), (0, 1))
    for h in (1, 2):
        for half in range(2):
            to_sibling(h, half).wait_recv()
    absorb(whole(1, 1), (0, 1))
    absorb(whole(1, 2), (0, 1))
    to_sibling(3, 0).wait_recv()
    absorb(((0, 3, 0), (1, 3, 0)), (0, 1))
    arrivals((2,), 2)
    to_sibling(3, 1).wait_recv()
    absorb(((0, 3, 1), (1, 3, 1)), (0, 1),
           steps=((1, HALF, HALF), (0, HALF, HALF), (1, 0, HALF), (0, 0, HALF)))

    back[0, 0:SLICE, :] = coded[0, 0:SLICE, :]
    back_pay[0, 0] = pay[0, 0]
    block = lax.broadcasted_iota(jnp.int32, (2, HALF), 1) // SLICE
    dens_rows = [None, None]
    for half in (1, 0):
        cols = slice(half * HALF, (half + 1) * HALF)
        placed = []
        for side in range(2):
            got = jnp.zeros((2, HALF), F32)
            for j in range(4):
                s = 4 * half + j
                if leaves(side, s):
                    give_pay(side, s).wait_recv()
                got = jnp.where(block == j, back_pay[side, s], got)
            dens_rows[half] = got[0:1, :] if side == 0 else dens_rows[half] + got[0:1, :]
            placed.append((perm_t[:, cols] * got[1:2, :]).astype(BF16))
        placed = jnp.concatenate(placed, axis=1)
        for side in range(2):
            for s in range(4 * half, 4 * half + 4):
                if leaves(side, s):
                    give_back(side, s).wait_recv()
        for part in range(3):
            at = slice(part * 256, (part + 1) * 256)
            value = jnp.concatenate([back[side, cols, at].astype(jnp.int32).astype(F32) for side in range(2)], axis=0)
            high = value.astype(BF16)
            low = (value - high.astype(F32)).astype(BF16)
            add = jnp.dot(placed, high, preferred_element_type=F32) + jnp.dot(
                placed, low, preferred_element_type=F32)
            out_ref[:, at] = add if half else out_ref[:, at] + add
    dens_row = jnp.concatenate(dens_rows, axis=1)
    d1 = dens_row.astype(BF16)
    rest = dens_row - d1.astype(F32)
    d2 = rest.astype(BF16)
    d3 = (rest - d2.astype(F32)).astype(BF16)
    lift = lambda v: jnp.broadcast_to(v.astype(F32), (16, ROWS))
    which = lax.broadcasted_iota(jnp.int32, (16, ROWS), 0)
    terms = jnp.where(which == 0, lift(d1), jnp.where(which == 1, lift(d2), jnp.where(which == 2, lift(d3), F32(0.0))))
    spread = jnp.dot(terms.astype(BF16), perm[...], preferred_element_type=F32)
    dens_ref[...] = jnp.sum(spread, axis=0, keepdims=True)

    for s in range(4, 8):
        deliver(s).wait_send()
    for side in range(2):
        for s in range(8):
            if leaves(side, s):
                give_back(side, s).wait_send()
                give_pay(side, s).wait_send()
    for g in range(3):
        over_link(SPLIT, 0, g).wait_send()
        for b in range(2):
            for k in range(3):
                over_link(b, k, g).wait_send()
    for h in range(4):
        for half in range(2):
            to_sibling(h, half).wait_send()


def on_device(embeddings, cluster_ids):
    dma = pltpu.SemaphoreType.DMA
    total, dens = pl.pallas_call(
        kernel,
        out_shape=(jax.ShapeDtypeStruct((ROWS, D), F32), jax.ShapeDtypeStruct((1, ROWS), F32)),
        in_specs=[pl.BlockSpec(memory_space=pltpu.HBM)] * 2,
        out_specs=(pl.BlockSpec(memory_space=pltpu.VMEM), pl.BlockSpec(memory_space=pltpu.VMEM)),
        scratch_shapes=[
            pltpu.VMEM((ROWS, D), BF16),
            pltpu.VMEM((1, ROWS), jnp.int32),
            dma((2,)),
            pltpu.VMEM((ROWS, D), BF16),
            pltpu.VMEM((2, 4, ROWS, D), BF16),
            pltpu.VMEM((ROWS, D), BF16),
            pltpu.VMEM((2 * ROWS, D), F32),
            pltpu.VMEM((2 * ROWS, 128), F32),
            pltpu.VMEM((ROWS, ROWS), BF16),
            pltpu.VMEM((ROWS, ROWS), F32),
            pltpu.VMEM((2 * ROWS, 128), F32),
            pltpu.VMEM((2, ROWS, D), jnp.int16),
            pltpu.VMEM((2, 2, 2, HALF), F32),
            pltpu.VMEM((2, ROWS, D), jnp.int16),
            pltpu.VMEM((2, 8, 2, HALF), F32),
            dma((8,)), dma((8,)),
            dma((3, 3, 3)), dma((3, 3, 3)),
            dma((4, 2)), dma((4, 2)),
            dma((2, 8)), dma((2, 8)),
            dma((2, 8)), dma((2, 8)),
        ],
        compiler_params=pltpu.CompilerParams(
            collective_id=0, has_side_effects=True, vmem_limit_bytes=40 * 1024 * 1024),
        cost_estimate=pl.CostEstimate(
            flops=4 * ROWS * 4096 * D, bytes_accessed=3 * ROWS * D * 2, transcendentals=ROWS * 4096),
    )(pltpu.with_memory_space_constraint(embeddings, pltpu.HBM), pltpu.with_memory_space_constraint(cluster_ids.reshape(1, ROWS), pltpu.HBM))
    return total, dens.reshape(ROWS)


def solution(mesh):
    in_specs = (P(("gr", "gc"), None), P(("gr", "gc")))
    out_specs = (P(("gr", "gc"), None), P(("gr", "gc")))
    return jax.shard_map(
        on_device, mesh=mesh, in_specs=in_specs, out_specs=out_specs, check_vma=False
    )
```

time: 336 us -> 46.2 us (0.14)
  waiting for transfers between devices: 152 us -> 0 us
  blocking collectives: 108 us -> 0 us
  matrix products: 53.7 us -> 0 us
  Pallas kernels: 0 us -> 44 us
  between operations: 14.4 us -> 0.64 us
  other arithmetic: 6.67 us -> 0 us
    all_gather x2 -> x0, waiting for transfers between devices: 93.9 us -> none  [the longest x1 64.1 us: on_device(): lax.all_gather(embeddings, 'gc', axis=0, tiled=True)]
    unnamed x1 -> x0, blocking collectives: 61.6 us -> none
    reduce_scatter x1 -> x0, waiting for transfers between devices: 56.5 us -> none  [on_device(): lax.psum_scatter(total, 'gc', scatter_dimension=0, tiled=True)]
    dot_general x2 -> x0, matrix products: 53.7 us -> none  [the longest x1 28.3 us: kernel_terms(): total = jnp.dot(coef, cols, preferred_element_type=jnp.float32)]
    all_gather x2 -> x0, blocking collectives: 46 us -> none  [the longest x1 28.5 us: on_device(): lax.all_gather(cluster_ids, 'gc', axis=0, tiled=True)]
    pallas_call x0 -> x1, Pallas kernels: none -> 44 us  [on_device(): pl.pallas_call(kernel, out_shape=(jax.ShapeDtypeStruct((ROWS, D), F32), j...]
    reduce_sum x2 -> x0, other arithmetic: 6.66 us -> none  [inverse_norms(): return lax.rsqrt(jnp.sum(wide * wide, axis=1) + 1e-06)]
  transfers between devices with their start and end apart: 3 -> 0, of which waited for: 3 -> 0; matrix products, arithmetic and copies ran while one was open for 1% -> 0% of each run, Pallas kernels for 0% -> 0%
where the time goes in v2:
time: 46.2 us; the launch traced here: 46.1 us
  Pallas kernels  44 us (95%)
  local copies, waits for them, and re-layouts  1.44 us (3%)
  between operations  0.64 us (1%)
    pallas_call x1, Pallas kernels, on_device(): pl.pallas_call(kernel, out_shape=(jax.ShapeDtypeStruct((ROWS, D), F32), j...  44 us
    unnamed x2, local copies, waits for them, and re-layouts  1.44 us

profile of v2, /device:TPU:1, one launch (start us, length us, event | category | flops | bytes accessed | tf_op | source)
XLA Modules:
  0.0 46.1 jit_solution(2671730868883005420)
XLA Ops:
  0.6 44.0 %shard_map.41 = (f32[256,768]{1,0:T(8,128)S(1)}, f32[1,256]{1,0:T(1,128)S(1)}) custom-call(bf16[256,768]{1,0:T(8,128)(2,1)} %e_hbm.1, s32[1,256]{1,0:T(1,128)} %bitcast.3), custom_call_target="tpu_custom_call" | custom-call | flops 3221225472 | bytes 1179648 | tf_op jit(solution)/shard_map/pallas_call | solution.py:322
  44.7 0.9 %copy.6 = f32[256,768]{1,0:T(8,128)} copy(f32[256,768]{1,0:T(8,128)S(1)} %get-tuple-element.8) | data formatting | bytes 1572864
  45.5 0.6 %copy.7 = f32[256]{0:T(256)} copy(f32[256]{0:T(256)S(1)} %bitcast.2) | data formatting | bytes 2048

commit v3 on v2

--- a/solution.py
+++ b/solution.py
@@ -28,19 +28,23 @@
     x = gc // 4
     y = ((gc // 2) % 2) * 2 + gr % 2
     z = gr // 2
-    return x, y, z, gc % 2
-
-
-def device(x, y, z, core):
+    return y, z, x, gc % 2
+
+
+def device(y, z, x, core):
     return (z * 2 + y % 2, x * 4 + (y // 2) * 2 + core)
 
 
 def near(v):
+    return 3 - v
+
+
+def far(v):
     return v + 1 - 2 * (v % 2)
 
 
-def far(v):
-    return 3 - v
+def block_bit(v):
+    return (v // 2 + v % 2) % 2
 
 
 ITEMS = (((0, 0), (1, 0), (1, 2)), ((1, 0), (0, 0), (0, 1)))
@@ -60,8 +64,7 @@
     deliver_send, deliver_recv, link_send, link_recv, core_send, core_recv,
     ret_send, ret_recv, pay_send, pay_recv,
 ):
-    x, y, z, core = place()
-    here = (x, y, z)
+    *here, core = place()
     outer = []
     for s in range(8):
         t = [far(here[a]) if (ORDER[s] >> a) & 1 else here[a] for a in range(3)]
@@ -70,7 +73,7 @@
     for a in range(3):
         t = [near(here[i]) if i == a else here[i] for i in range(3)]
         inner.append(device(*t, core))
-    sibling = device(x, y, z, 1 - core)
+    sibling = device(*here, 1 - core)
     across = []
     for s in range(8):
         t = [far(here[a]) if (ORDER[s] >> a) & 1 else here[a] for a in range(3)]
@@ -87,7 +90,7 @@
     for load in loads:
         load.start()
 
-    mine = x // 2 + 2 * (y // 2) + 4 * (z // 2)
+    mine = block_bit(here[0]) + 2 * block_bit(here[1]) + 4 * block_bit(here[2])
     loads[0].wait()
     rel = jnp.bitwise_xor(ids_ref[...], mine)
     slot = jnp.where(rel == 3, 4, jnp.where(rel == 4, 3, rel)).astype(F32)
@@ -100,26 +103,26 @@
     perm[...] = p
     loads[1].wait()
     rows = jnp.dot(p, e_ref[...], preferred_element_type=F32).astype(BF16)
-    sorted_ref[...] = rows
-    held[0, 0, 0:SLICE, :] = rows[0:SLICE]
+    for part in range(PARTS):
+        sorted_ref[part] = rows[:, part * W:(part + 1) * W]
+        held[0, 0, part, 0:SLICE, :] = rows[0:SLICE, part * W:(part + 1) * W]
 
     pl.semaphore_wait(barrier, 18)
 
     def deliver(s):
         return pltpu.make_async_remote_copy(
-            src_ref=sorted_ref.at[pl.ds(s * SLICE, SLICE), :],
-            dst_ref=held.at[0, 0, pl.ds(s * SLICE, SLICE), :],
+            src_ref=sorted_ref.at[:, pl.ds(s * SLICE, SLICE), :],
+            dst_ref=held.at[0, 0, :, pl.ds(s * SLICE, SLICE), :],
             send_sem=deliver_send.at[s], recv_sem=deliver_recv.at[s],
             device_id=outer[s], device_id_type=MESH)
 
     def over_link(b, k, g):
         rows = pl.ds(*GROUPS[g])
         if b == SPLIT:
-            source, target = held.at[0, 0, rows, :], across_rows.at[rows, :]
+            source, target = held.at[0, 0, :, rows, :], across_rows.at[:, rows, :]
         else:
             part, h = ITEMS[b][k]
-            cols = pl.ds(part * W, W)
-            source, target = held.at[0, h, rows, cols], held.at[0, h ^ (1 << b), rows, cols]
+            source, target = held.at[0, h, part, rows, :], held.at[0, h ^ (1 << b), part, rows, :]
         return pltpu.make_async_remote_copy(
             src_ref=source, dst_ref=target,
             send_sem=link_send.at[b, k, g], recv_sem=link_recv.at[b, k, g],
@@ -128,14 +131,14 @@
     def to_sibling(h, half):
         rows = pl.ds(half * HALF, HALF)
         return pltpu.make_async_remote_copy(
-            src_ref=held.at[0, h, rows, :], dst_ref=held.at[1, h, rows, :],
+            src_ref=held.at[0, h, :, rows, :], dst_ref=held.at[1, h, :, rows, :],
             send_sem=core_send.at[h, half], recv_sem=core_recv.at[h, half],
             device_id=sibling, device_id_type=MESH)
 
     def piece_to_sibling(part, h, g):
-        rows, cols = pl.ds(*GROUPS[g]), pl.ds(part * W, W)
-        return pltpu.make_async_remote_copy(
-            src_ref=held.at[0, h, rows, cols], dst_ref=held.at[1, h, rows, cols],
+        rows = pl.ds(*GROUPS[g])
+        return pltpu.make_async_remote_copy(
+            src_ref=held.at[0, h, part, rows, :], dst_ref=held.at[1, h, part, rows, :],
             send_sem=core_send.at[h, g // 2], recv_sem=core_recv.at[h, g // 2],
             device_id=sibling, device_id_type=MESH)
 
@@ -152,12 +155,15 @@
         return lax.rsqrt(jnp.sum(wide * wide, axis=1, keepdims=True) + 1e-06)
 
     def absorb(pieces, sides, first=False, steps=None):
-        cols = jnp.concatenate([held[c, h, half * HALF:(half + 1) * HALF, :] for c, h, half in pieces], axis=0)
+        cols = jnp.concatenate([
+            jnp.concatenate([held[c, h, part, half * HALF:(half + 1) * HALF, :] for part in range(PARTS)], axis=1)
+            for c, h, half in pieces], axis=0)
         inv_lanes = to_lanes(row_inv(cols))
         for side, start, size in steps or [(side, 0, ROWS) for side in sides]:
             own = slice(start, start + size)
             rows = slice(side * ROWS + start, side * ROWS + start + size)
-            mine = held[0, 0, own, :] if side == 0 else across_rows[own, :]
+            mine = jnp.concatenate([
+                held[0, 0, part, own, :] if side == 0 else across_rows[part, own, :] for part in range(PARTS)], axis=1)
             if first:
                 inv_ref[rows, :] = jnp.broadcast_to(row_inv(mine), (size, 128))
             raw = lax.dot_general(mine, cols, (((1,), (1,)), ((), ())), preferred_element_type=F32)
@@ -328,9 +334,9 @@
             pltpu.VMEM((ROWS, D), BF16),
             pltpu.VMEM((1, ROWS), jnp.int32),
             dma((2,)),
-            pltpu.VMEM((ROWS, D), BF16),
-            pltpu.VMEM((2, 4, ROWS, D), BF16),
-            pltpu.VMEM((ROWS, D), BF16),
+            pltpu.VMEM((PARTS, ROWS, W), BF16),
+            pltpu.VMEM((2, 4, PARTS, ROWS, W), BF16),
+            pltpu.VMEM((PARTS, ROWS, W), BF16),
             pltpu.VMEM((2 * ROWS, D), F32),
             pltpu.VMEM((2 * ROWS, 128), F32),
             pltpu.VMEM((ROWS, ROWS), BF16),

time: 46.2 us -> 44.8 us (0.970)
  Pallas kernels: 44 us -> 42.6 us
    pallas_call x1, Pallas kernels: 44 us -> 42.6 us  [on_device(): pl.pallas_call(kernel, out_shape=(jax.ShapeDtypeStruct((ROWS, D), F32), j...]
where the time goes in v3:
time: 44.8 us; the launch traced here: 44.7 us
  Pallas kernels  42.6 us (95%)
  local copies, waits for them, and re-layouts  1.44 us (3%)
  between operations  0.64 us (1%)
    pallas_call x1, Pallas kernels, on_device(): pl.pallas_call(kernel, out_shape=(jax.ShapeDtypeStruct((ROWS, D), F32), j...  42.6 us
    unnamed x2, local copies, waits for them, and re-layouts  1.44 us

profile of v3, /device:TPU:1, one launch (start us, length us, event | category | flops | bytes accessed | tf_op | source)
XLA Modules:
  0.0 44.7 jit_solution(1791522980171280861)
XLA Ops:
  0.6 42.6 %shard_map.41 = (f32[256,768]{1,0:T(8,128)S(1)}, f32[1,256]{1,0:T(1,128)S(1)}) custom-call(bf16[256,768]{1,0:T(8,128)(2,1)} %e_hbm.1, s32[1,256]{1,0:T(1,128)} %bitcast.3), custom_call_target="tpu_custom_call" | custom-call | flops 3221225472 | bytes 1179648 | tf_op jit(solution)/shard_map/pallas_call | solution.py:328
  43.2 0.9 %copy.6 = f32[256,768]{1,0:T(8,128)} copy(f32[256,768]{1,0:T(8,128)S(1)} %get-tuple-element.8) | data formatting | bytes 1572864
  44.1 0.6 %copy.7 = f32[256]{0:T(256)} copy(f32[256]{0:T(256)S(1)} %bitcast.2) | data formatting | bytes 2048

commit v4 on v3

--- a/solution.py
+++ b/solution.py
@@ -323,6 +323,14 @@
             to_sibling(h, half).wait_send()
 
 
+def write_out(total, dens, total_out, dens_out, sems):
+    copies = [pltpu.make_async_copy(total, total_out, sems.at[0]), pltpu.make_async_copy(dens, dens_out, sems.at[1])]
+    for copy in copies:
+        copy.start()
+    for copy in copies:
+        copy.wait()
+
+
 def on_device(embeddings, cluster_ids):
     dma = pltpu.SemaphoreType.DMA
     total, dens = pl.pallas_call(
@@ -357,6 +365,14 @@
         cost_estimate=pl.CostEstimate(
             flops=4 * ROWS * 4096 * D, bytes_accessed=3 * ROWS * D * 2, transcendentals=ROWS * 4096),
     )(pltpu.with_memory_space_constraint(embeddings, pltpu.HBM), pltpu.with_memory_space_constraint(cluster_ids.reshape(1, ROWS), pltpu.HBM))
+    total, dens = pl.pallas_call(
+        write_out,
+        out_shape=(jax.ShapeDtypeStruct((ROWS, D), F32), jax.ShapeDtypeStruct((1, ROWS), F32)),
+        in_specs=[pl.BlockSpec(memory_space=pltpu.VMEM)] * 2,
+        out_specs=(pl.BlockSpec(memory_space=pl.ANY), pl.BlockSpec(memory_space=pl.ANY)),
+        scratch_shapes=[dma((2,))],
+        compiler_params=pltpu.CompilerParams(vmem_limit_bytes=4 * 1024 * 1024),
+    )(total, dens)
     return total, dens.reshape(ROWS)
 
 

time: 44.8 us -> 44.3 us (0.989)
  local copies, waits for them, and re-layouts: 1.44 us -> 0 us
  Pallas kernels: 42.6 us -> 43.5 us
    unnamed x2 -> x0, local copies, waits for them, and re-layouts: 1.44 us -> none
    pallas_call x0 -> x1, Pallas kernels: none -> 0.9 us  [on_device(): pl.pallas_call(write_out, out_shape=(jax.ShapeDtypeStruct((ROWS, D), F32)...]
where the time goes in v4:
time: 44.3 us; the launch traced here: 44.1 us
  Pallas kernels  43.5 us (98%)
  between operations  0.64 us (1%)
    pallas_call x1, Pallas kernels, on_device(): pl.pallas_call(kernel, out_shape=(jax.ShapeDtypeStruct((ROWS, D), F32), j...  42.6 us
    pallas_call x1, Pallas kernels, on_device(): pl.pallas_call(write_out, out_shape=(jax.ShapeDtypeStruct((ROWS, D), F32)...  0.9 us

profile of v4, /device:TPU:1, one launch (start us, length us, event | category | flops | bytes accessed | tf_op | source)
XLA Modules:
  0.0 44.1 jit_solution(14152423589870894754)
XLA Ops:
  0.6 42.6 %shard_map.41 = (f32[256,768]{1,0:T(8,128)S(1)}, f32[1,256]{1,0:T(1,128)S(1)}) custom-call(bf16[256,768]{1,0:T(8,128)(2,1)} %e_hbm.1, s32[1,256]{1,0:T(1,128)} %bitcast.2), custom_call_target="tpu_custom_call" | custom-call | flops 3221225472 | bytes 1179648 | tf_op jit(solution)/shard_map/pallas_call | solution.py:336
  43.2 0.9 %shard_map.42 = (f32[256,768]{1,0:T(8,128)}, f32[1,256]{1,0:T(1,128)}) custom-call(f32[256,768]{1,0:T(8,128)S(1)} %get-tuple-element.6.total, f32[1,256]{1,0:T(1,128)S(1)} %get-tuple-element.7.dens), custom_call_target="tpu_custom_call" | custom-call | tf_op jit(solution)/shard_map/pallas_call | solution.py:368

commit v5 on v4

--- a/solution.py
+++ b/solution.py
@@ -119,6 +119,7 @@
     def over_link(b, k, g):
         rows = pl.ds(*GROUPS[g])
         if b == SPLIT:
+            rows = pl.ds((g - 1) * HALF, HALF)
             source, target = held.at[0, 0, :, rows, :], across_rows.at[:, rows, :]
         else:
             part, h = ITEMS[b][k]
@@ -215,7 +216,7 @@
         for k in range(2):
             for b in range(2):
                 over_link(b, k, g).start()
-            if k == 0:
+            if k == 0 and g > 0:
                 over_link(SPLIT, 0, g).start()
 
     def arrivals(ks, g):
@@ -247,7 +248,7 @@
     to_sibling(0, 1).wait_recv()
     absorb(whole(1, 0), (0,))
     arrivals((2,), 1)
-    for g in range(3):
+    for g in range(1, 3):
         over_link(SPLIT, 0, g).wait_recv()
     absorb(whole(0, 0), (1,), first=True)
     arrivals(range(2), 2)
@@ -314,7 +315,8 @@
                 give_back(side, s).wait_send()
                 give_pay(side, s).wait_send()
     for g in range(3):
-        over_link(SPLIT, 0, g).wait_send()
+        if g > 0:
+            over_link(SPLIT, 0, g).wait_send()
         for b in range(2):
             for k in range(3):
                 over_link(b, k, g).wait_send()

time: 44.3 us -> 44.3 us (level)
  no operation moved by 1% of the time
where the time goes in v5:
time: 44.3 us; the launch traced here: 44.1 us
  Pallas kernels  43.5 us (98%)
  between operations  0.64 us (1%)
    pallas_call x1, Pallas kernels, on_device(): pl.pallas_call(kernel, out_shape=(jax.ShapeDtypeStruct((ROWS, D), F32), j...  42.6 us
    pallas_call x1, Pallas kernels, on_device(): pl.pallas_call(write_out, out_shape=(jax.ShapeDtypeStruct((ROWS, D), F32)...  0.9 us

profile of v5, /device:TPU:1, one launch (start us, length us, event | category | flops | bytes accessed | tf_op | source)
XLA Modules:
  0.0 44.1 jit_solution(3166695125690322744)
XLA Ops:
  0.6 42.6 %shard_map.41 = (f32[256,768]{1,0:T(8,128)S(1)}, f32[1,256]{1,0:T(1,128)S(1)}) custom-call(bf16[256,768]{1,0:T(8,128)(2,1)} %e_hbm.1, s32[1,256]{1,0:T(1,128)} %bitcast.2), custom_call_target="tpu_custom_call" | custom-call | flops 3221225472 | bytes 1179648 | tf_op jit(solution)/shard_map/pallas_call | solution.py:338
  43.2 0.9 %shard_map.42 = (f32[256,768]{1,0:T(8,128)}, f32[1,256]{1,0:T(1,128)}) custom-call(f32[256,768]{1,0:T(8,128)S(1)} %get-tuple-element.6.total, f32[1,256]{1,0:T(1,128)S(1)} %get-tuple-element.7.dens), custom_call_target="tpu_custom_call" | custom-call | tf_op jit(solution)/shard_map/pallas_call | solution.py:370
